TPU v7x, 256 devices: a whole 4x4x8 slice. The times are simulated.
256 devices in a mesh: ctx: 32 (over x, z), cls: 8 (over y, core).
Axes of the slice: x: 4, y: 4, z: 8, core: 2. Of those that a mesh axis runs over, the one named last changes fastest.
Arguments:
- tokens: bfloat16 [196608, 8192], P(('ctx', 'cls')), may hold values from -80 to 80
- doc_length: int32 [1], replicated, may hold values from 98304 to 196608
- queries: bfloat16 [64, 8192], P('cls', 'ctx'), may hold values from -0.046875 to 0.046875
- norm_gain: float32 [8192], P('ctx'), may hold values from 0.1 to 1.9
- head_weight: bfloat16 [8192, 4096], P('ctx', 'cls'), may hold values from -0.0625 to 0.0625
- head_bias: float32 [4096], P('cls'), may hold values from -20 to 20
- labels: int32 [4096], P('cls'), may hold values 0 or 1
Outputs:
- mean_loss: float32 [], replicated
- query_grad: float32 [64, 8192], P('cls', 'ctx')
- head_grad: float32 [8192, 4096], P('ctx', 'cls')
- bias_grad: float32 [4096], P('cls')
All inputs are finite; a program needn't handle non-finite values. No bound on the sum of `labels` on one device may be relied on, other than what follows from the above.
Results may differ from a plain program's by a relative error of at most 0.017.
Values may be sent and summed in bfloat16 or wider, within the bound.
A program may use at most 64 MiB of HBM per device.

v0:
```python
import jax
import jax.numpy as jnp
from jax import lax
from jax.sharding import PartitionSpec as P


def shards(tokens, doc_length, queries, norm_gain, head_weight, head_bias, labels):
    context_count = lax.axis_size("ctx")
    class_count = lax.axis_size("cls")
    context_index = lax.axis_index("ctx")
    class_index = lax.axis_index("cls")
    token_count = tokens.shape[0]
    query_share = queries.shape[0]
    width_share = queries.shape[1]
    full_width = width_share * context_count

    def project_add(block_piece):
        return lax.dot_general(
            block_piece, tokens, (((1,), (1,)), ((), ())), preferred_element_type=jnp.float32
        )

    query_block = lax.all_gather(queries, "cls", axis=0, tiled=True)
    scores = project_add(lax.all_gather(query_block, "ctx", axis=1, tiled=True))
    offset = (context_index * class_count + class_index) * token_count
    position = offset + jnp.arange(token_count, dtype=jnp.int32)
    valid_mask = (position < doc_length[0])[None, :]
    local_peak = jnp.max(jnp.where(valid_mask, scores, -1e30), axis=1)
    peak = lax.pmax(local_peak, ("ctx", "cls"))
    weights = jnp.exp(jnp.where(valid_mask, scores - peak[:, None], -1e30))
    pooled_part = jnp.dot(weights.astype(jnp.bfloat16), tokens, preferred_element_type=jnp.float32)
    whole_sum = lax.psum(pooled_part, ("ctx", "cls"))
    pooled = lax.dynamic_slice(
        whole_sum,
        (class_index * query_share, context_index * width_share),
        (query_share, width_share),
    )
    scaled_b = (pooled * norm_gain[None, :]).astype(jnp.bfloat16)
    head_blocks = head_weight.reshape(width_share, query_share, -1)
    square_part = jnp.sum(pooled * pooled, axis=1)
    logit_part = jnp.einsum("hd,dha->ha", scaled_b, head_blocks, preferred_element_type=jnp.float32)
    squares, logit_raw = lax.psum((square_part, logit_part), "ctx")
    inverse_rms = lax.rsqrt(squares / full_width + 1e-05)
    logits = inverse_rms[:, None] * logit_raw + head_bias.reshape(query_share, -1)
    target = labels.reshape(query_share, -1).astype(jnp.float32)
    loss_part = jnp.sum(jax.nn.softplus(logits) - target * logits)
    mean_loss = lax.psum(loss_part, "cls") / (labels.shape[0] * class_count)
    logit_grad = jax.nn.sigmoid(logits) - target
    normed = pooled * inverse_rms[:, None] * norm_gain[None, :]
    head_grad = jnp.einsum("hd,ha->dha", normed, logit_grad).reshape(width_share, -1)
    normed_grad = (
        jnp.einsum("dha,ha->hd", head_blocks.astype(jnp.float32), logit_grad) * norm_gain[None, :]
    )
    unit_pooled = pooled * inverse_rms[:, None]
    inner_part = jnp.sum(unit_pooled * normed_grad, axis=1)
    inner_mean = lax.psum(inner_part, "ctx") / full_width
    pooled_grad = (inverse_rms[:, None] * (normed_grad - unit_pooled * inner_mean[:, None])).astype(
        jnp.bfloat16
    )
    grad_block = lax.all_gather(pooled_grad, "cls", axis=0, tiled=True)
    projected = project_add(lax.all_gather(grad_block, "ctx", axis=1, tiled=True))
    score_grad = (weights * projected).astype(jnp.bfloat16)
    query_part = jnp.dot(score_grad, tokens, preferred_element_type=jnp.float32)
    column_grad = lax.psum_scatter(query_part, "ctx", scatter_dimension=1, tiled=True)
    query_grad = lax.psum_scatter(column_grad, "cls", scatter_dimension=0, tiled=True)
    return (mean_loss, query_grad, head_grad, logit_grad.reshape(-1))


def solution(mesh):
    return jax.shard_map(
        shards,
        mesh=mesh,
        in_specs=(
            P(("ctx", "cls"), None),
            P(),
            P("cls", "ctx"),
            P("ctx"),
            P("ctx", "cls"),
            P("cls"),
            P("cls"),
        ),
        out_specs=(P(), P("cls", "ctx"), P("ctx", "cls"), P("cls")),
        check_vma=False,
    )
```

profile of v0, /device:TPU:2, one launch (start us, length us, event | category | flops | bytes accessed | tf_op | source)
XLA Modules:
  0.0 943.6 jit_solution(2797138843445842792)
XLA Ops:
  7.2 0.0 all-gather.3.cloned.1.call-start
  7.2 14.3 %all_gather.12 = bf16[64,256]{1,0:T(8,128)(2,1)} all-gather(bf16[8,256]{1,0:T(8,128)(2,1)} %param.9), channel_id=1, replica_groups=mesh['ctx'=32,'cls'=8] {'cls'}, dimensions={0}, use_global_device_ids=true | all-gather | bytes 36864 | tf_op jit(solution)/shard_map/all_gather | solution.py:22
  21.5 0.0 all-gather.3.cloned.1.call-update
  21.6 0.0 all-reduce.3.cloned.1.call-start
  22.3 72.8 %all-gather.3.cloned.1.call-done = bf16[64,8192]{1,0:T(8,128)(2,1)} async-done(((bf16[64,256]{1,0:T(8,128)(2,1)}), bf16[64,8192]{1,0:T(8,128)(2,1)}) %all-gather.3.cloned.1.call-update) | async-done | bytes 1048592 | tf_op jit(solution)/shard_map/all_gather | solution.py:23
  95.0 8.9 select_reduce_fusion
  104.0 74.6 %pmax.7 = f32[64]{0:T(128)S(1)} all-reduce(f32[64]{0:T(128)S(1)} %get-tuple-element.16), channel_id=1, replica_groups=mesh['ctx'=32,'cls'=8] {'ctx','cls'}, use_global_device_ids=true, to_apply=%region_1.2 | all-reduce | flops 64 | bytes 512 | tf_op jit(solution)/shard_map/pmax | solution.py:28
  178.6 8.2 fusion.3
  186.9 0.0 all-gather.5.cloned.1.call-start
  187.0 0.1 copy.12
  187.1 0.1 convert_element_type.22
  187.2 0.1 reshape.32
  187.3 257.2 %all-reduce.3.cloned.1.call-done = f32[64,8192]{1,0:T(8,128)} async-done(((f32[64,8192]{1,0:T(8,128)}), f32[64,8192]{1,0:T(8,128)}) %all-reduce.3.cloned.1.call-update) | async-done | bytes 2097168 | tf_op jit(solution)/shard_map/psum | solution.py:31
  444.5 0.8 multiply_reduce_fusion.1
  445.3 0.2 fusion.11
  445.5 61.5 %all-reduce = (f32[8,64]{1,0:T(8,128)S(1)}, f32[8]{0:T(128)S(1)}) all-reduce(f32[8,64]{1,0:T(8,128)S(1)} %bitcast.32, f32[8]{0:T(128)S(1)} %get-tuple-element.12), channel_id=1, replica_groups=mesh['ctx'=32,'cls'=8] {'ctx'}, use_global_device_ids=true, to_apply=%region_5.6 | all-reduce | flops 520 | bytes 4160 | tf_op jit(solution)/shard_map/psum | solution.py:41
  507.0 0.7 divide_subtract_fusion
  507.7 0.1 fusion.18
  507.8 0.9 multiply_multiply_fusion
  508.7 69.2 %psum.39 = f32[8]{0:T(128)S(1)} all-reduce(f32[8]{0:T(128)S(1)} %get-tuple-element.11), channel_id=1, replica_groups=mesh['ctx'=32,'cls'=8] {'ctx'}, use_global_device_ids=true, to_apply=%region_9.10 | all-reduce | flops 8 | bytes 64 | tf_op jit(solution)/shard_map/psum | solution.py:55
  577.9 0.8 multiply_convert_fusion
  578.7 13.7 %all_gather.14 = bf16[64,256]{1,0:T(8,128)(2,1)} all-gather(bf16[8,256]{1,0:T(8,128)(2,1)S(1)} %multiply_convert_fusion), channel_id=1, replica_groups=mesh['ctx'=32,'cls'=8] {'cls'}, dimensions={0}, use_global_device_ids=true | all-gather | bytes 36864 | tf_op jit(solution)/shard_map/all_gather | solution.py:59
  592.4 0.2 reduce-scatter.3.cloned.1.call-start
  592.6 76.7 %all-gather.5.cloned.1.call-done = bf16[64,8192]{1,0:T(8,128)(2,1)} async-done(((bf16[64,256]{1,0:T(8,128)(2,1)}), bf16[64,8192]{1,0:T(8,128)(2,1)}) %all-gather.5.cloned.1.call-update) | async-done | bytes 1048592 | tf_op jit(solution)/shard_map/all_gather | solution.py:60
  669.4 17.7 %fusion.1 = f32[64,8192]{1,0:T(8,128)} fusion(bf16[768,8192]{1,0:T(8,128)(2,1)} %param.7, bf16[64,8192]{1,0:T(8,128)(2,1)} %all-gather.5.cloned.1.call-done, f32[64,768]{1,0:T(8,128)S(1)} %get-tuple-element.17, f32[64]{0:T(128)S(1)} %pmax.7, pred[768]{0:T(1024)(128)(4,1)S(1)} %add_compare_fusion), kind=kOutput, calls=%fused_computation.2 | convolution fusion | flops 1610809344 | bytes 15926272 | tf_op jit(solution)/shard_map/dot_general | solution.py:62
  687.1 0.0 reduce-scatter.5.cloned.1.call-start
  687.2 13.1 %psum.38 = f32[]{:T(128)} all-reduce(f32[]{:T(128)} %get-tuple-element.15), channel_id=1, replica_groups=mesh['ctx'=32,'cls'=8] {'cls'}, use_global_device_ids=true, to_apply=%region_7.8 | all-reduce | flops 1 | bytes 8 | tf_op jit(solution)/shard_map/psum | solution.py:46
  700.2 0.7 reshape.34
  700.9 200.1 %reduce-scatter.3.cloned.1.call-done = f32[64,256]{1,0:T(8,128)} async-done(((f32[64,8192]{1,0:T(8,128)}), f32[64,256]{1,0:T(8,128)}) %reduce-scatter.3.cloned.1.call-update) | async-done | bytes 65552 | tf_op jit(solution)/shard_map/reduce_scatter | solution.py:63
  901.0 0.1 broadcast_multiply_fusion
  901.1 1.0 copy.13
  902.8 33.2 %reduce-scatter.5.cloned.1.call-done = f32[8,256]{1,0:T(8,128)} async-done(((f32[64,256]{1,0:T(8,128)}), f32[8,256]{1,0:T(8,128)}) %reduce-scatter.5.cloned.1.call-update) | async-done | bytes 8208 | tf_op jit(solution)/shard_map/reduce_scatter | solution.py:64
  (16 shorter events, 0.1 us)
Async XLA Ops:
  7.2 87.9 %all-gather.3.cloned.1.call-start = ((), (), s32[]{:S(2)}) async-start(), calls=%async_computation.2 | async-start | bytes 1081344 | tf_op jit(solution)/shard_map/all_gather | solution.py:23
  21.6 422.9 %all-reduce.3.cloned.1.call-start = ((), (), s32[]{:S(2)}) async-start(), calls=%async_computation.3 | async-start | bytes 4194304 | tf_op jit(solution)/shard_map/psum | solution.py:31
  104.0 83.0 %copy-start = (bf16[256,512]{1,0:T(8,128)(2,1)S(1)}, bf16[256,512]{1,0:T(8,128)(2,1)}, u32[]{:S(2)}) copy-start(bf16[256,512]{1,0:T(8,128)(2,1)} %param.11) | copy-start | bytes 786436
  104.0 83.1 %copy-start.3 = (s32[512]{0:T(512)S(1)}, s32[512]{0:T(512)}, u32[]{:S(2)}) copy-start(s32[512]{0:T(512)} %param.13) | copy-start | bytes 6148
  104.0 83.2 %copy-start.2 = (f32[512]{0:T(512)S(1)}, f32[512]{0:T(512)}, u32[]{:S(2)}) copy-start(f32[512]{0:T(512)} %param.12) | copy-start | bytes 6148
  104.0 340.5 %copy-start.1 = (f32[256]{0:T(256)S(1)}, f32[256]{0:T(256)}, u32[]{:S(2)}) copy-start(f32[256]{0:T(256)} %param.10) | copy-start | bytes 3076
  186.9 482.5 %all-gather.5.cloned.1.call-start = ((), (), s32[]{:S(2)}) async-start(), calls=%async_computation.4 | async-start | bytes 1081344 | tf_op jit(solution)/shard_map/all_gather | solution.py:60
  592.4 308.6 %reduce-scatter.3.cloned.1.call-start = ((), (), s32[]{:S(2)}) async-start(), calls=%async_computation.5 | async-start | bytes 2162688 | tf_op jit(solution)/shard_map/reduce_scatter | solution.py:63
  687.1 248.9 %reduce-scatter.5.cloned.1.call-start = ((), (), s32[]{:S(2)}) async-start(), calls=%async_computation.6 | async-start | bytes 73728 | tf_op jit(solution)/shard_map/reduce_scatter | solution.py:64
Sparse Core Ops, SparseCore 0:
  21.7 73.3 all-gather.2
  187.0 257.4 all-reduce.2
  592.5 76.7 all-gather.4
  687.2 213.7 reduce-scatter.2
  904.0 31.8 reduce-scatter.4
where the time goes:
time: 944 us
  waiting for transfers between devices  640 us (68%)
  blocking collectives  246 us (26%)
  matrix products  35.2 us (4%)
  between operations  16.3 us (2%)
    psum x1, waiting for transfers between devices, shards(): whole_sum = lax.psum(pooled_part, ('ctx', 'cls'))  257 us
    reduce_scatter x1, waiting for transfers between devices, shards(): lax.psum_scatter(query_part, 'ctx', scatter_dimension=1, tiled=True)  200 us
    all_gather x1, waiting for transfers between devices, shards(): lax.all_gather(grad_block, 'ctx', axis=1, tiled=True)  76.7 us
    pmax x1, blocking collectives, shards(): peak = lax.pmax(local_peak, ('ctx', 'cls'))  74.6 us
    all_gather x1, waiting for transfers between devices, shards(): scores = project_add(lax.all_gather(query_block, 'ctx', axis=1, tiled=True))  72.8 us
    psum x1, blocking collectives, shards(): inner_mean = lax.psum(inner_part, 'ctx') / full_width  69.2 us
    psum x1, blocking collectives, shards(): squares, logit_raw = lax.psum((square_part, logit_part), 'ctx')  61.5 us
    reduce_scatter x1, waiting for transfers between devices, shards(): lax.psum_scatter(column_grad, 'cls', scatter_dimension=0, tiled=True)  33.2 us
  transfers between devices with their start and end apart: 5, of which 5 were waited for; matrix products, arithmetic and copies ran while one was open for 0% of the time, Pallas kernels for 0%

commit v1 on v0

--- a/solution.py
+++ b/solution.py
@@ -28,7 +28,7 @@
     peak = lax.pmax(local_peak, ("ctx", "cls"))
     weights = jnp.exp(jnp.where(valid_mask, scores - peak[:, None], -1e30))
     pooled_part = jnp.dot(weights.astype(jnp.bfloat16), tokens, preferred_element_type=jnp.float32)
-    whole_sum = lax.psum(pooled_part, ("ctx", "cls"))
+    whole_sum = lax.psum(lax.psum(pooled_part, "cls"), "ctx")
     pooled = lax.dynamic_slice(
         whole_sum,
         (class_index * query_share, context_index * width_share),

time: 944 us -> 913 us (0.967)
  waiting for transfers between devices: 640 us -> 606 us
    psum x1 -> x2, waiting for transfers between devices: 257 us -> 223 us  [shards(): whole_sum = lax.psum(lax.psum(pooled_part, 'cls'), 'ctx')]
  transfers between devices with their start and end apart: 5 -> 6, of which waited for: 5 -> 6; matrix products, arithmetic and copies ran while one was open for 0% -> 0% of each run, Pallas kernels for 0% -> 0%
where the time goes in v1:
time: 913 us; the launch traced here: 912 us
  waiting for transfers between devices  606 us (66%)
  blocking collectives  248 us (27%)
  matrix products  35.2 us (4%)
  between operations  16.7 us (2%)
    psum x2, waiting for transfers between devices, shards(): whole_sum = lax.psum(lax.psum(pooled_part, 'cls'), 'ctx')  223 us
    reduce_scatter x1, waiting for transfers between devices, shards(): lax.psum_scatter(query_part, 'ctx', scatter_dimension=1, tiled=True)  200 us
    all_gather x1, waiting for transfers between devices, shards(): lax.all_gather(grad_block, 'ctx', axis=1, tiled=True)  77.6 us
    pmax x1, blocking collectives, shards(): peak = lax.pmax(local_peak, ('ctx', 'cls'))  74.6 us
    all_gather x1, waiting for transfers between devices, shards(): scores = project_add(lax.all_gather(query_block, 'ctx', axis=1, tiled=True))  72.8 us
    psum x1, blocking collectives, shards(): inner_mean = lax.psum(inner_part, 'ctx') / full_width  68.5 us
    psum x1, blocking collectives, shards(): squares, logit_raw = lax.psum((square_part, logit_part), 'ctx')  63.7 us
    reduce_scatter x1, waiting for transfers between devices, shards(): lax.psum_scatter(column_grad, 'cls', scatter_dimension=0, tiled=True)  33 us
  transfers between devices with their start and end apart: 6, of which 6 were waited for; matrix products, arithmetic and copies ran while one was open for 0% of the time, Pallas kernels for 0%

profile of v1, /device:TPU:2, one launch (start us, length us, event | category | flops | bytes accessed | tf_op | source)
XLA Modules:
  0.0 912.1 jit_solution(15196408127941569957)
XLA Ops:
  7.2 14.3 %all_gather.12 = bf16[64,256]{1,0:T(8,128)(2,1)} all-gather(bf16[8,256]{1,0:T(8,128)(2,1)} %param.9), channel_id=1, replica_groups=mesh['ctx'=32,'cls'=8] {'cls'}, dimensions={0}, use_global_device_ids=true | all-gather | bytes 36864 | tf_op jit(solution)/shard_map/all_gather | solution.py:22
  21.6 0.0 all-reduce.4.cloned.1.call-start
  22.3 72.8 %all-gather.3.cloned.1.call-done = bf16[64,8192]{1,0:T(8,128)(2,1)} async-done(((bf16[64,256]{1,0:T(8,128)(2,1)}), bf16[64,8192]{1,0:T(8,128)(2,1)}) %all-gather.3.cloned.1.call-update) | async-done | bytes 1048592 | tf_op jit(solution)/shard_map/all_gather | solution.py:23
  95.0 8.9 select_reduce_fusion
  104.0 74.6 %pmax.7 = f32[64]{0:T(128)S(1)} all-reduce(f32[64]{0:T(128)S(1)} %get-tuple-element.16), channel_id=1, replica_groups=mesh['ctx'=32,'cls'=8] {'ctx','cls'}, use_global_device_ids=true, to_apply=%region_1.2 | all-reduce | flops 64 | bytes 512 | tf_op jit(solution)/shard_map/pmax | solution.py:28
  178.7 8.2 fusion.3
  186.9 0.0 all-reduce.6.cloned.1.call-start
  187.0 67.1 %all-reduce.4.cloned.1.call-done = f32[64,8192]{1,0:T(8,128)} async-done(((f32[64,8192]{1,0:T(8,128)}), f32[64,8192]{1,0:T(8,128)}) %all-reduce.4.cloned.1.call-update) | async-done | bytes 2097168 | tf_op jit(solution)/shard_map/psum | solution.py:31
  254.1 0.0 all-gather.5.cloned.1.call-start
  254.2 0.1 copy.12
  254.3 0.1 convert_element_type.22
  254.4 0.1 reshape.32
  254.5 155.5 %all-reduce.6.cloned.1.call-done = f32[64,8192]{1,0:T(8,128)} async-done(((f32[64,8192]{1,0:T(8,128)}), f32[64,8192]{1,0:T(8,128)}) %all-reduce.6.cloned.1.call-update) | async-done | bytes 2097168 | tf_op jit(solution)/shard_map/psum | solution.py:31
  410.0 0.8 multiply_reduce_fusion.1
  410.8 0.2 fusion.11
  411.0 63.7 %all-reduce = (f32[8,64]{1,0:T(8,128)S(1)}, f32[8]{0:T(128)S(1)}) all-reduce(f32[8,64]{1,0:T(8,128)S(1)} %bitcast.32, f32[8]{0:T(128)S(1)} %get-tuple-element.12), channel_id=1, replica_groups=mesh['ctx'=32,'cls'=8] {'ctx'}, use_global_device_ids=true, to_apply=%region_6.7 | all-reduce | flops 520 | bytes 4160 | tf_op jit(solution)/shard_map/psum | solution.py:41
  474.7 0.7 divide_subtract_fusion
  475.4 0.1 fusion.18
  475.5 0.9 multiply_multiply_fusion
  476.4 68.5 %psum.47 = f32[8]{0:T(128)S(1)} all-reduce(f32[8]{0:T(128)S(1)} %get-tuple-element.11), channel_id=1, replica_groups=mesh['ctx'=32,'cls'=8] {'ctx'}, use_global_device_ids=true, to_apply=%region_10.11 | all-reduce | flops 8 | bytes 64 | tf_op jit(solution)/shard_map/psum | solution.py:55
  545.0 0.8 multiply_convert_fusion
  545.7 14.0 %all_gather.14 = bf16[64,256]{1,0:T(8,128)(2,1)} all-gather(bf16[8,256]{1,0:T(8,128)(2,1)S(1)} %multiply_convert_fusion), channel_id=1, replica_groups=mesh['ctx'=32,'cls'=8] {'cls'}, dimensions={0}, use_global_device_ids=true | all-gather | bytes 36864 | tf_op jit(solution)/shard_map/all_gather | solution.py:59
  559.8 0.2 reduce-scatter.3.cloned.1.call-start
  560.0 77.6 %all-gather.5.cloned.1.call-done = bf16[64,8192]{1,0:T(8,128)(2,1)} async-done(((bf16[64,256]{1,0:T(8,128)(2,1)}), bf16[64,8192]{1,0:T(8,128)(2,1)}) %all-gather.5.cloned.1.call-update) | async-done | bytes 1048592 | tf_op jit(solution)/shard_map/all_gather | solution.py:60
  637.6 17.7 %fusion.1 = f32[64,8192]{1,0:T(8,128)} fusion(bf16[768,8192]{1,0:T(8,128)(2,1)} %param.7, bf16[64,8192]{1,0:T(8,128)(2,1)} %all-gather.5.cloned.1.call-done, f32[64,768]{1,0:T(8,128)S(1)} %get-tuple-element.17, f32[64]{0:T(128)S(1)} %pmax.7, pred[768]{0:T(1024)(128)(4,1)S(1)} %add_compare_fusion), kind=kOutput, calls=%fused_computation.2 | convolution fusion | flops 1610809344 | bytes 15926272 | tf_op jit(solution)/shard_map/dot_general | solution.py:62
  655.4 0.0 reduce-scatter.5.cloned.1.call-start
  655.4 13.1 %psum.46 = f32[]{:T(128)} all-reduce(f32[]{:T(128)} %get-tuple-element.15), channel_id=1, replica_groups=mesh['ctx'=32,'cls'=8] {'cls'}, use_global_device_ids=true, to_apply=%region_8.9 | all-reduce | flops 1 | bytes 8 | tf_op jit(solution)/shard_map/psum | solution.py:46
  668.5 0.7 reshape.34
  669.1 200.2 %reduce-scatter.3.cloned.1.call-done = f32[64,256]{1,0:T(8,128)} async-done(((f32[64,8192]{1,0:T(8,128)}), f32[64,256]{1,0:T(8,128)}) %reduce-scatter.3.cloned.1.call-update) | async-done | bytes 65552 | tf_op jit(solution)/shard_map/reduce_scatter | solution.py:63
  869.3 0.1 broadcast_multiply_fusion
  869.4 1.0 copy.13
  871.1 33.0 %reduce-scatter.5.cloned.1.call-done = f32[8,256]{1,0:T(8,128)} async-done(((f32[64,256]{1,0:T(8,128)}), f32[8,256]{1,0:T(8,128)}) %reduce-scatter.5.cloned.1.call-update) | async-done | bytes 8208 | tf_op jit(solution)/shard_map/reduce_scatter | solution.py:64
  (19 shorter events, 0.2 us)
Async XLA Ops:
  7.2 87.9 %all-gather.3.cloned.1.call-start = ((), (), s32[]{:S(2)}) async-start(), calls=%async_computation.2 | async-start | bytes 1081344 | tf_op jit(solution)/shard_map/all_gather | solution.py:23
  21.6 232.5 %all-reduce.4.cloned.1.call-start = ((), (), s32[]{:S(2)}) async-start(), calls=%async_computation.3 | async-start | bytes 4194304 | tf_op jit(solution)/shard_map/psum | solution.py:31
  104.0 150.2 %copy-start = (bf16[256,512]{1,0:T(8,128)(2,1)S(1)}, bf16[256,512]{1,0:T(8,128)(2,1)}, u32[]{:S(2)}) copy-start(bf16[256,512]{1,0:T(8,128)(2,1)} %param.11) | copy-start | bytes 786436
  104.0 150.3 %copy-start.3 = (s32[512]{0:T(512)S(1)}, s32[512]{0:T(512)}, u32[]{:S(2)}) copy-start(s32[512]{0:T(512)} %param.13) | copy-start | bytes 6148
  104.0 150.4 %copy-start.2 = (f32[512]{0:T(512)S(1)}, f32[512]{0:T(512)}, u32[]{:S(2)}) copy-start(f32[512]{0:T(512)} %param.12) | copy-start | bytes 6148
  104.0 306.0 %copy-start.1 = (f32[256]{0:T(256)S(1)}, f32[256]{0:T(256)}, u32[]{:S(2)}) copy-start(f32[256]{0:T(256)} %param.10) | copy-start | bytes 3076
  186.9 223.1 %all-reduce.6.cloned.1.call-start = ((), (), s32[]{:S(2)}) async-start(), calls=%async_computation.4 | async-start | bytes 4194304 | tf_op jit(solution)/shard_map/psum | solution.py:31
  254.1 383.5 %all-gather.5.cloned.1.call-start = ((), (), s32[]{:S(2)}) async-start(), calls=%async_computation.5 | async-start | bytes 1081344 | tf_op jit(solution)/shard_map/all_gather | solution.py:60
  559.8 309.5 %reduce-scatter.3.cloned.1.call-start = ((), (), s32[]{:S(2)}) async-start(), calls=%async_computation.6 | async-start | bytes 2162688 | tf_op jit(solution)/shard_map/reduce_scatter | solution.py:63
  655.4 248.8 %reduce-scatter.5.cloned.1.call-start = ((), (), s32[]{:S(2)}) async-start(), calls=%async_computation.7 | async-start | bytes 73728 | tf_op jit(solution)/shard_map/reduce_scatter | solution.py:64
Sparse Core Ops, SparseCore 0:
  21.7 73.3 all-gather.2
  187.0 66.9 all-reduce.3
  257.6 152.3 all-reduce.5
  559.9 77.6 all-gather.4
  655.5 213.7 reduce-scatter.2
  872.2 31.8 reduce-scatter.4
